TPU v7x, 32 devices: a whole 2x2x4 slice. The times are simulated.
32 devices in a mesh: video: 2 (over x), frame: 4 (over z), head: 4 (over y, core).
Axes of the slice: x: 2, y: 2, z: 4, core: 2. Of those that a mesh axis runs over, the one named last changes fastest.
Arguments:
- latents: bfloat16 [2048, 2560], P(('video', 'frame', 'head')), parts along dimension 0, may hold values from -24 to 24
- weights: bfloat16 [2560, 3, 2560], P(None, None, 'head'), may hold values from -0.125 to 0.125
- key_slots: int32 [16, 4, 4], P('frame'), may hold values from 0 to 3, as said below
- key_count: int32 [16, 4], P('frame'), may hold values from 0 to 4, as said below
Outputs:
- attended: bfloat16 [2048, 2560], P(('video', 'frame'), 'head'), parts along dimension 0
There are 2 independent parts, one for each index of `video`. A program takes and returns all parts, laid end to end along the dimension named above; an argument that names none is the same for every part. Nothing has to cross between parts.
Inputs may be any that keep to these rules, and one draw needn't show every extreme that they name: key_slots[a, b, :] is a permutation of the local block numbers of a slab. key_count[a, b] is 4 when query block a lies in slab b; otherwise it is at most max(1, 4 // p), where p is the largest power of two not above the distance between a's slab and b.
All inputs are finite; a program needn't handle non-finite values.
Results may differ from a plain program's by a relative error of at most 0.012.
The roundings to bfloat16 on the way count: a program that leaves them out, or rounds other values in their place, can miss the bound.
Values may be sent and summed in bfloat16 or wider, within the bound.
A program may use at most 128 MiB of HBM per device.

v0:
```python
import jax
import jax.numpy as jnp
from jax import lax
from jax.sharding import PartitionSpec as P

HD = 128
masked_score = -1e30


def on_device(latents, weights, key_slots, key_count):
    width_in = weights.shape[0]
    local_width = weights.shape[2]
    w_joined = weights.reshape(width_in, 3 * local_width)
    joined = jnp.dot(
        lax.all_gather(latents, "head", axis=0, tiled=True),
        w_joined,
        preferred_element_type=jnp.float32,
    ).astype(jnp.bfloat16)
    slab_len = joined.shape[0]
    head_count = local_width // HD
    query_heads = joined[:, :local_width].reshape(slab_len, head_count, HD)
    keys_here = joined[:, local_width : 2 * local_width]
    values_here = joined[:, 2 * local_width :]
    score_scale = HD ** (-0.5)
    blocks_here = key_slots.shape[0]
    slab_total = key_slots.shape[1]
    per_slab = key_slots.shape[2]
    block_rows = slab_len // blocks_here
    all_blocks = slab_total * per_slab
    block_ids = jnp.arange(per_slab, dtype=jnp.int32)
    listed = jnp.any(
        (key_slots[:, :, :, None] == block_ids[None, None, None, :])
        & (block_ids[None, None, :, None] < key_count[:, :, None, None]),
        axis=2,
    )
    allowed = listed.reshape(blocks_here, all_blocks).astype(jnp.float32)

    def compute(state, key_part, value_part, visible):
        row_count = key_part.shape[0]
        top_score, denominator, numerator = state
        scores = (
            jnp.einsum(
                "qhd,khd->hqk",
                query_heads,
                key_part.reshape(row_count, head_count, HD),
                preferred_element_type=jnp.float32,
            )
            * score_scale
        )
        scores = jnp.where(visible[None], scores, masked_score)
        new_top = jnp.maximum(top_score, jnp.max(scores, axis=-1))
        rescale = jnp.exp(top_score - new_top)
        shares = jnp.exp(scores - new_top[:, :, None])
        denominator = denominator * rescale + jnp.sum(shares, axis=-1)
        update = jnp.einsum(
            "hqk,khd->qhd",
            shares.astype(jnp.bfloat16),
            value_part.reshape(row_count, head_count, HD),
            preferred_element_type=jnp.float32,
        )
        numerator = numerator * jnp.transpose(rescale)[:, :, None] + update
        return (new_top, denominator, numerator)

    def attend_rows(running, key_part, value_part, first_row):
        row_count = key_part.shape[0]
        row_blocks = (first_row + jnp.arange(row_count, dtype=jnp.int32)) // block_rows
        onehot = (jnp.arange(all_blocks, dtype=jnp.int32)[:, None] == row_blocks[None, :]).astype(
            jnp.float32
        )
        listed_here = jnp.dot(allowed, onehot) > 0.5
        visible = jnp.broadcast_to(
            listed_here[:, None, :], (blocks_here, block_rows, row_count)
        ).reshape(slab_len, row_count)
        return compute(running, key_part, value_part, visible)

    initial = (
        jnp.full((head_count, slab_len), masked_score, jnp.float32),
        jnp.zeros((head_count, slab_len), jnp.float32),
        jnp.zeros((slab_len, head_count, HD), jnp.float32),
    )
    key_part = lax.all_gather(keys_here, "frame", axis=0, tiled=True)
    value_part = lax.all_gather(values_here, "frame", axis=0, tiled=True)
    row_count = key_part.shape[0]
    step_rows = 512

    def one_block(position, state):
        key_block = lax.dynamic_slice_in_dim(key_part, position * step_rows, step_rows, 0)
        value_block = lax.dynamic_slice_in_dim(value_part, position * step_rows, step_rows, 0)
        return attend_rows(state, key_block, value_block, position * step_rows)

    running = lax.fori_loop(0, row_count // step_rows, one_block, initial)
    top_score, denominator, numerator = running
    mixed = numerator / jnp.transpose(denominator)[:, :, None]
    return mixed.reshape(slab_len, local_width).astype(jnp.bfloat16)


def solution(mesh):
    return jax.shard_map(
        on_device,
        mesh=mesh,
        in_specs=(
            P(("video", "frame", "head"), None),
            P(None, None, "head"),
            P("frame", None, None),
            P("frame", None),
        ),
        out_specs=P(("video", "frame"), "head"),
        check_vma=False,
    )
```

profile of v0, /device:TPU:0, one launch (start us, length us, event | category | flops | bytes accessed | tf_op | source)
XLA Modules:
  0.0 130.2 jit_solution(18211134643761131619)
XLA Ops:
  6.5 0.7 all-gather.4.cloned.1.call-update
  7.3 13.8 %copy.22 = bf16[2560,3,640]{0,2,1:T(8,128)(2,1)} copy(bf16[2560,3,640]{2,0,1:T(8,128)(2,1)} %param.7) | data formatting | bytes 19660800 | tf_op args[1]
  21.1 8.7 %all-gather.4.cloned.1.call-done = bf16[256,2560]{1,0:T(8,128)(2,1)} async-done(((bf16[64,2560]{1,0:T(8,128)(2,1)}), bf16[256,2560]{1,0:T(8,128)(2,1)}) %all-gather.4.cloned.1.call-update) | async-done | bytes 1310736 | tf_op jit(solution)/shard_map/all_gather | solution.py:15
  29.8 7.1 %convolution_convert_fusion = bf16[256,1920]{1,0:T(8,128)(2,1)S(1)} fusion(bf16[256,2560]{1,0:T(8,128)(2,1)} %all-gather.4.cloned.1.call-done, bf16[2560,1920]{0,1:T(8,128)(2,1)} %bitcast.63), kind=kOutput, calls=%fused_computation.35 | convolution fusion | flops 2517073920 | bytes 12124160 | tf_op jit(solution)/shard_map/dot_general | solution.py:14
  37.0 0.9 fusion.26
  38.0 0.7 all-gather.8.cloned.1.call-update
  38.7 0.1 iota_compare_fusion.3
  38.8 0.1 fusion.25
  38.9 0.1 reshape.69
  39.0 0.2 copy.23
  39.2 0.9 copy.25
  40.1 30.7 %all-gather.6.cloned.1.call-done = bf16[1024,640]{1,0:T(8,128)(2,1)} async-done(((bf16[256,640]{1,0:T(8,128)(2,1)}), bf16[1024,640]{1,0:T(8,128)(2,1)}) %all-gather.6.cloned.1.call-update) | async-done | bytes 1310736 | tf_op jit(solution)/shard_map/all_gather | solution.py:81
  70.8 33.3 %all-gather.8.cloned.1.call-done = bf16[1024,640]{1,0:T(8,128)(2,1)} async-done(((bf16[256,640]{1,0:T(8,128)(2,1)}), bf16[1024,640]{1,0:T(8,128)(2,1)}) %all-gather.8.cloned.1.call-update) | async-done | bytes 1310736 | tf_op jit(solution)/shard_map/all_gather | solution.py:82
  104.1 17.6 %while.20 = (s32[]{:T(128)}, f32[5,256]{1,0:T(8,128)S(1)}, f32[5,256]{1,0:T(8,128)S(1)}, f32[256,5,128]{0,2,1:T(8,128)}, bf16[4,16]{1,0:T(4,128)(2,1)S(1)}, /*in...) while((s32[]{:T(128)}, f32[5,256]{1,0:T(8,128)S(1)}, ...), condition=%wide.region_4.5_spmd.clone, body=%wide.region_1.4_spmd.clone.sunk | while | flops 343336448 | bytes 16933176 | solution.py:91
  104.1 2.2 %constant_dynamic-slice_fusion.3 = (bf16[512,640]{1,0:T(8,128)(2,1)}, bf16[512,640]{1,0:T(8,128)(2,1)S(1)}) fusion(bf16[1024,640]{1,0:T(8,128)(2,1)} %get-tuple-element.375, s32[]{:T(128)S(6)} %select_n.63, bf16[1024,640]{1,0:T(8,128)(2,1)} %get-tuple-element.373), kind=kLoop, calls=%fused_computation.31.clone.1 | loop fusion | bytes 2621444 | tf_op jit(solution)/shard_map/while/body/eval_jaxpr/dynamic_slice | solution.py:88
  106.3 0.2 copy.36
  106.6 0.1 fusion.49
  106.8 0.3 copy.35
  107.0 1.6 %fusion.50 = (f32[5,256]{1,0:T(8,128)S(1)}, f32[5,512,256]{2,1,0:T(8,128)S(1)}) fusion(pred[256,512]{0,1:T(8,128)(4,1)S(1)} %copy.35, bf16[512,5,128]{0,2,1:T(8,128)(2,1)S(1)} %bitcast.60, bf16[256,5,128]{2,0,1:T(8,128)(2,1)} %get-tuple-element.374), kind=kOutput, calls=%fused_computation.4.clone.1 | convolution fusion | flops 169736960 | bytes 3740672 | tf_op jit(solution)/shard_map/while/body/eval_jaxpr/qhd,khd->hqk/dot_general | solution.py:42
  108.7 1.3 %copy.37 = bf16[512,640]{0,1:T(8,128)(2,1)S(1)} copy(bf16[512,640]{1,0:T(8,128)(2,1)} %get-tuple-element.342) | data formatting | bytes 1310720 | tf_op jit(solution)/shard_map/while/body/eval_jaxpr/dynamic_slice | solution.py:88
  110.0 1.7 %fusion.54 = f32[256,5,128]{0,2,1:T(8,128)} fusion(bf16[512,5,128]{0,2,1:T(8,128)(2,1)S(1)} %bitcast.61, f32[5,512,256]{2,1,0:T(8,128)S(1)} %get-tuple-element.341, f32[5,256]{1,0:T(8,128)S(1)} %get-tuple-element.369, pred[256,512]{0,1:T(8,128)(4,1)S(1)} %copy.35, f32[256,5,128]{0,2,1:T(8,128)} %get-tuple-element.359, ...), kind=kOutput, calls=%fused_computation.11.clone.1 | convolution fusion | flops 170885120 | bytes 4728833 | tf_op jit(solution)/shard_map/while/body/eval_jaxpr/hqk,khd->qhd/dot_general | solution.py:55
  111.7 0.6 fusion.52
  112.3 2.2 %constant_dynamic-slice_fusion.3 = (bf16[512,640]{1,0:T(8,128)(2,1)}, bf16[512,640]{1,0:T(8,128)(2,1)S(1)}) fusion(bf16[1024,640]{1,0:T(8,128)(2,1)} %get-tuple-element.375, s32[]{:T(128)S(6)} %select_n.63, bf16[1024,640]{1,0:T(8,128)(2,1)} %get-tuple-element.373), kind=kLoop, calls=%fused_computation.31.clone.1 | loop fusion | bytes 2621444 | tf_op jit(solution)/shard_map/while/body/eval_jaxpr/dynamic_slice | solution.py:88
  114.6 0.2 copy.36
  114.8 0.1 fusion.49
  115.0 0.3 copy.35
  115.3 1.6 %fusion.50 = (f32[5,256]{1,0:T(8,128)S(1)}, f32[5,512,256]{2,1,0:T(8,128)S(1)}) fusion(pred[256,512]{0,1:T(8,128)(4,1)S(1)} %copy.35, bf16[512,5,128]{0,2,1:T(8,128)(2,1)S(1)} %bitcast.60, bf16[256,5,128]{2,0,1:T(8,128)(2,1)} %get-tuple-element.374), kind=kOutput, calls=%fused_computation.4.clone.1 | convolution fusion | flops 169736960 | bytes 3740672 | tf_op jit(solution)/shard_map/while/body/eval_jaxpr/qhd,khd->hqk/dot_general | solution.py:42
  116.9 1.3 %copy.37 = bf16[512,640]{0,1:T(8,128)(2,1)S(1)} copy(bf16[512,640]{1,0:T(8,128)(2,1)} %get-tuple-element.342) | data formatting | bytes 1310720 | tf_op jit(solution)/shard_map/while/body/eval_jaxpr/dynamic_slice | solution.py:88
  118.3 2.8 %fusion.54 = f32[256,5,128]{0,2,1:T(8,128)} fusion(bf16[512,5,128]{0,2,1:T(8,128)(2,1)S(1)} %bitcast.61, f32[5,512,256]{2,1,0:T(8,128)S(1)} %get-tuple-element.341, f32[5,256]{1,0:T(8,128)S(1)} %get-tuple-element.369, pred[256,512]{0,1:T(8,128)(4,1)S(1)} %copy.35, f32[256,5,128]{0,2,1:T(8,128)} %get-tuple-element.359, ...), kind=kOutput, calls=%fused_computation.11.clone.1 | convolution fusion | flops 170885120 | bytes 4728833 | tf_op jit(solution)/shard_map/while/body/eval_jaxpr/hqk,khd->qhd/dot_general | solution.py:55
  121.0 0.6 fusion.52
  121.6 1.1 divide_convert_fusion
  122.8 0.9 copy.27
  (22 shorter events, 0.3 us)
Async XLA Ops:
  6.5 23.3 %all-gather.4.cloned.1.call-start = ((), (), s32[]{:S(2)}) async-start(), calls=%async_computation | async-start | bytes 1638400 | tf_op jit(solution)/shard_map/all_gather | solution.py:15
  7.3 63.5 %all-gather.6.cloned.1.call-start = ((), (), s32[]{:S(2)}) async-start(), calls=%async_computation.1 | async-start | bytes 1638400 | tf_op jit(solution)/shard_map/all_gather | solution.py:81
  36.9 1.7 %copy-start.1 = (s32[4,4]{1,0:T(4,128)S(1)}, s32[4,4]{1,0:T(4,128)}, u32[]{:S(2)}) copy-start(s32[4,4]{1,0:T(4,128)} %param.9) | copy-start | bytes 196
  37.0 1.8 %copy-start = (s32[4,4,4]{2,1,0:T(4,128)S(1)}, s32[4,4,4]{2,1,0:T(4,128)}, u32[]{:S(2)}) copy-start(s32[4,4,4]{2,1,0:T(4,128)} %param.8) | copy-start | bytes 772
  37.9 66.2 %all-gather.8.cloned.1.call-start = ((), (), s32[]{:S(2)}) async-start(), calls=%async_computation.2 | async-start | bytes 1638400 | tf_op jit(solution)/shard_map/all_gather | solution.py:82
Sparse Core Ops, SparseCore 0:
  8.9 20.8 all-gather.3
  38.0 32.6 all-gather.5
  72.3 31.6 all-gather.7
where the time goes:
time: 131 us; the launch traced here: 130 us
  waiting for transfers between devices  74.1 us (57%)
  local copies, waits for them, and re-layouts  25.1 us (19%)
  matrix products  15.1 us (12%)
  between operations  13.2 us (10%)
  other arithmetic  2.52 us (2%)
    all_gather x1, waiting for transfers between devices, on_device(): value_part = lax.all_gather(values_here, 'frame', axis=0, tiled=True)  33.3 us
    all_gather x1, waiting for transfers between devices, on_device(): key_part = lax.all_gather(keys_here, 'frame', axis=0, tiled=True)  30.7 us
    unnamed x6, local copies, waits for them, and re-layouts  14.7 us
    all_gather x1, waiting for transfers between devices, on_device(): lax.all_gather(latents, 'head', axis=0, tiled=True)  8.7 us
    dynamic_slice x4, local copies, waits for them, and re-layouts, one_block(): lax.dynamic_slice_in_dim(value_part, position * step_rows, step_rows, 0)  7.14 us
    dot_general x1, matrix products, on_device(): jnp.dot(lax.all_gather(latents, 'head', axis=0, tiled=True), w_joined, pr...  7.09 us
    dot_general x2, matrix products, compute(): jnp.einsum('hqk,khd->qhd', shares.astype(jnp.bfloat16), value_part.reshap...  4.46 us
    dot_general x2, matrix products, compute(): jnp.einsum('qhd,khd->hqk', query_heads, key_part.reshape(row_count, head_...  3.27 us
  transfers between devices with their start and end apart: 3, of which 3 were waited for; matrix products, arithmetic and copies ran while one was open for 12% of the time, Pallas kernels for 0%

commit v1 on v0

--- a/solution.py
+++ b/solution.py
@@ -78,8 +78,13 @@
         jnp.zeros((head_count, slab_len), jnp.float32),
         jnp.zeros((slab_len, head_count, HD), jnp.float32),
     )
-    key_part = lax.all_gather(keys_here, "frame", axis=0, tiled=True)
-    value_part = lax.all_gather(values_here, "frame", axis=0, tiled=True)
+    key_part, value_part = jnp.split(
+        lax.all_gather(
+            jnp.concatenate([keys_here, values_here], axis=1), "frame", axis=0, tiled=True
+        ),
+        [keys_here.shape[1]],
+        axis=1,
+    )
     row_count = key_part.shape[0]
     step_rows = 512
 

time: 131 us -> 124 us (0.947)
  waiting for transfers between devices: 74.1 us -> 62.9 us
  local copies, waits for them, and re-layouts: 25.1 us -> 28.5 us
    all_gather x2 -> x1, waiting for transfers between devices: 64 us -> 53.5 us  [on_device(): lax.all_gather(jnp.concatenate([keys_here, values_here], axis=1), 'frame'...]
    split x0 -> x1, local copies, waits for them, and re-layouts: none -> 3.44 us  [on_device(): jnp.split(lax.all_gather(jnp.concatenate([keys_here, values_here], axis=1...]
  transfers between devices with their start and end apart: 3 -> 2, of which waited for: 3 -> 2; matrix products, arithmetic and copies ran while one was open for 12% -> 12% of each run, Pallas kernels for 0% -> 0%
where the time goes in v1:
time: 124 us; the launch traced here: 123 us
  waiting for transfers between devices  62.9 us (51%)
  local copies, waits for them, and re-layouts  28.5 us (23%)
  matrix products  15.2 us (12%)
  between operations  13.5 us (11%)
  other arithmetic  2.52 us (2%)
    all_gather x1, waiting for transfers between devices, on_device(): lax.all_gather(jnp.concatenate([keys_here, values_here], axis=1), 'frame'...  53.5 us
    unnamed x6, local copies, waits for them, and re-layouts  14.8 us
    all_gather x1, waiting for transfers between devices, on_device(): lax.all_gather(latents, 'head', axis=0, tiled=True)  8.69 us
    dynamic_slice x4, local copies, waits for them, and re-layouts, one_block(): lax.dynamic_slice_in_dim(value_part, position * step_rows, step_rows, 0)  7.16 us
    dot_general x1, matrix products, on_device(): jnp.dot(lax.all_gather(latents, 'head', axis=0, tiled=True), w_joined, pr...  7.12 us
    dot_general x2, matrix products, compute(): jnp.einsum('hqk,khd->qhd', shares.astype(jnp.bfloat16), value_part.reshap...  4.52 us
    split x1, local copies, waits for them, and re-layouts, on_device(): jnp.split(lax.all_gather(jnp.concatenate([keys_here, values_here], axis=1...  3.44 us
    dot_general x2, matrix products, compute(): jnp.einsum('qhd,khd->hqk', query_heads, key_part.reshape(row_count, head_...  3.27 us
  transfers between devices with their start and end apart: 2, of which 2 were waited for; matrix products, arithmetic and copies ran while one was open for 12% of the time, Pallas kernels for 0%

profile of v1, /device:TPU:0, one launch (start us, length us, event | category | flops | bytes accessed | tf_op | source)
XLA Modules:
  0.0 122.8 jit_solution(966911389424450713)
XLA Ops:
  6.5 0.7 all-gather.3.cloned.1.call-update
  7.3 0.0 all-gather.5.cloned.1.call-start
  7.3 13.9 %copy.22 = bf16[2560,3,640]{0,2,1:T(8,128)(2,1)} copy(bf16[2560,3,640]{2,0,1:T(8,128)(2,1)} %param.7) | data formatting | bytes 19660800 | tf_op args[1]
  21.2 8.7 %all-gather.3.cloned.1.call-done = bf16[256,2560]{1,0:T(8,128)(2,1)} async-done(((bf16[64,2560]{1,0:T(8,128)(2,1)}), bf16[256,2560]{1,0:T(8,128)(2,1)}) %all-gather.3.cloned.1.call-update) | async-done | bytes 1310736 | tf_op jit(solution)/shard_map/all_gather | solution.py:15
  29.8 7.1 %convolution_convert_fusion = bf16[256,1920]{1,0:T(8,128)(2,1)S(1)} fusion(bf16[256,2560]{1,0:T(8,128)(2,1)} %all-gather.3.cloned.1.call-done, bf16[2560,1920]{0,1:T(8,128)(2,1)} %bitcast.63), kind=kOutput, calls=%fused_computation.35 | convolution fusion | flops 2517073920 | bytes 12124160 | tf_op jit(solution)/shard_map/dot_general | solution.py:14
  37.0 0.9 concatenate.4
  37.9 0.1 iota_compare_fusion.3
  38.0 0.1 fusion.25
  38.1 0.1 reshape.69
  38.3 0.2 copy.23
  38.4 0.9 copy.25
  39.3 53.5 %all-gather.5.cloned.1.call-done = bf16[1024,1280]{1,0:T(8,128)(2,1)} async-done(((bf16[256,1280]{1,0:T(8,128)(2,1)}), bf16[1024,1280]{1,0:T(8,128)(2,1)}) %all-gather.5.cloned.1.call-update) | async-done | bytes 2621456 | tf_op jit(solution)/shard_map/all_gather | solution.py:82
  92.9 3.4 %fusion.26 = (bf16[1024,640]{1,0:T(8,128)(2,1)}, bf16[1024,640]{1,0:T(8,128)(2,1)}) fusion(bf16[1024,1280]{1,0:T(8,128)(2,1)} %all-gather.5.cloned.1.call-done), kind=kLoop, calls=%fused_computation.41 | loop fusion | bytes 5242880 | tf_op jit(solution)/shard_map/split | solution.py:81
  96.3 17.6 %while.20 = (s32[]{:T(128)}, f32[5,256]{1,0:T(8,128)S(1)}, f32[5,256]{1,0:T(8,128)S(1)}, f32[256,5,128]{0,2,1:T(8,128)}, bf16[4,16]{1,0:T(4,128)(2,1)S(1)}, /*in...) while((s32[]{:T(128)}, f32[5,256]{1,0:T(8,128)S(1)}, ...), condition=%wide.region_4.5_spmd.clone, body=%wide.region_1.4_spmd.clone.sunk | while | flops 343336448 | bytes 16933176 | solution.py:96
  96.3 2.2 %constant_dynamic-slice_fusion.3 = (bf16[512,640]{1,0:T(8,128)(2,1)}, bf16[512,640]{1,0:T(8,128)(2,1)S(1)}) fusion(bf16[1024,640]{1,0:T(8,128)(2,1)} %get-tuple-element.374, s32[]{:T(128)S(6)} %select_n.63, bf16[1024,640]{1,0:T(8,128)(2,1)} %get-tuple-element.372), kind=kLoop, calls=%fused_computation.31.clone.1 | loop fusion | bytes 2621444 | tf_op jit(solution)/shard_map/while/body/eval_jaxpr/dynamic_slice | solution.py:93
  98.5 0.2 copy.36
  98.8 0.1 fusion.49
  99.0 0.3 copy.35
  99.3 1.6 %fusion.50 = (f32[5,256]{1,0:T(8,128)S(1)}, f32[5,512,256]{2,1,0:T(8,128)S(1)}) fusion(pred[256,512]{0,1:T(8,128)(4,1)S(1)} %copy.35, bf16[512,5,128]{0,2,1:T(8,128)(2,1)S(1)} %bitcast.60, bf16[256,5,128]{2,0,1:T(8,128)(2,1)} %get-tuple-element.373), kind=kOutput, calls=%fused_computation.4.clone.1 | convolution fusion | flops 169736960 | bytes 3740672 | tf_op jit(solution)/shard_map/while/body/eval_jaxpr/qhd,khd->hqk/dot_general | solution.py:42
  100.9 1.3 %copy.37 = bf16[512,640]{0,1:T(8,128)(2,1)S(1)} copy(bf16[512,640]{1,0:T(8,128)(2,1)} %get-tuple-element.341) | data formatting | bytes 1310720 | tf_op jit(solution)/shard_map/while/body/eval_jaxpr/dynamic_slice | solution.py:93
  102.3 1.7 %fusion.54 = f32[256,5,128]{0,2,1:T(8,128)} fusion(bf16[512,5,128]{0,2,1:T(8,128)(2,1)S(1)} %bitcast.61, f32[5,512,256]{2,1,0:T(8,128)S(1)} %get-tuple-element.340, f32[5,256]{1,0:T(8,128)S(1)} %get-tuple-element.368, pred[256,512]{0,1:T(8,128)(4,1)S(1)} %copy.35, f32[256,5,128]{0,2,1:T(8,128)} %get-tuple-element.358, ...), kind=kOutput, calls=%fused_computation.11.clone.1 | convolution fusion | flops 170885120 | bytes 4728833 | tf_op jit(solution)/shard_map/while/body/eval_jaxpr/hqk,khd->qhd/dot_general | solution.py:55
  104.0 0.6 fusion.52
  104.6 2.2 %constant_dynamic-slice_fusion.3 = (bf16[512,640]{1,0:T(8,128)(2,1)}, bf16[512,640]{1,0:T(8,128)(2,1)S(1)}) fusion(bf16[1024,640]{1,0:T(8,128)(2,1)} %get-tuple-element.374, s32[]{:T(128)S(6)} %select_n.63, bf16[1024,640]{1,0:T(8,128)(2,1)} %get-tuple-element.372), kind=kLoop, calls=%fused_computation.31.clone.1 | loop fusion | bytes 2621444 | tf_op jit(solution)/shard_map/while/body/eval_jaxpr/dynamic_slice | solution.py:93
  106.8 0.2 copy.36
  107.1 0.1 fusion.49
  107.3 0.3 copy.35
  107.5 1.6 %fusion.50 = (f32[5,256]{1,0:T(8,128)S(1)}, f32[5,512,256]{2,1,0:T(8,128)S(1)}) fusion(pred[256,512]{0,1:T(8,128)(4,1)S(1)} %copy.35, bf16[512,5,128]{0,2,1:T(8,128)(2,1)S(1)} %bitcast.60, bf16[256,5,128]{2,0,1:T(8,128)(2,1)} %get-tuple-element.373), kind=kOutput, calls=%fused_computation.4.clone.1 | convolution fusion | flops 169736960 | bytes 3740672 | tf_op jit(solution)/shard_map/while/body/eval_jaxpr/qhd,khd->hqk/dot_general | solution.py:42
  109.2 1.3 %copy.37 = bf16[512,640]{0,1:T(8,128)(2,1)S(1)} copy(bf16[512,640]{1,0:T(8,128)(2,1)} %get-tuple-element.341) | data formatting | bytes 1310720 | tf_op jit(solution)/shard_map/while/body/eval_jaxpr/dynamic_slice | solution.py:93
  110.5 2.8 %fusion.54 = f32[256,5,128]{0,2,1:T(8,128)} fusion(bf16[512,5,128]{0,2,1:T(8,128)(2,1)S(1)} %bitcast.61, f32[5,512,256]{2,1,0:T(8,128)S(1)} %get-tuple-element.340, f32[5,256]{1,0:T(8,128)S(1)} %get-tuple-element.368, pred[256,512]{0,1:T(8,128)(4,1)S(1)} %copy.35, f32[256,5,128]{0,2,1:T(8,128)} %get-tuple-element.358, ...), kind=kOutput, calls=%fused_computation.11.clone.1 | convolution fusion | flops 170885120 | bytes 4728833 | tf_op jit(solution)/shard_map/while/body/eval_jaxpr/hqk,khd->qhd/dot_general | solution.py:55
  113.3 0.6 fusion.52
  113.9 1.1 divide_convert_fusion
  115.1 0.9 copy.27
  (21 shorter events, 0.2 us)
Async XLA Ops:
  6.5 23.3 %all-gather.3.cloned.1.call-start = ((), (), s32[]{:S(2)}) async-start(), calls=%async_computation | async-start | bytes 1638400 | tf_op jit(solution)/shard_map/all_gather | solution.py:15
  7.3 85.6 %all-gather.5.cloned.1.call-start = ((), (), s32[]{:S(2)}) async-start(), calls=%async_computation.1 | async-start | bytes 3276800 | tf_op jit(solution)/shard_map/all_gather | solution.py:82
  29.8 8.1 %copy-start.1 = (s32[4,4]{1,0:T(4,128)S(1)}, s32[4,4]{1,0:T(4,128)}, u32[]{:S(2)}) copy-start(s32[4,4]{1,0:T(4,128)} %param.9) | copy-start | bytes 196
  29.8 8.2 %copy-start = (s32[4,4,4]{2,1,0:T(4,128)S(1)}, s32[4,4,4]{2,1,0:T(4,128)}, u32[]{:S(2)}) copy-start(s32[4,4,4]{2,1,0:T(4,128)} %param.8) | copy-start | bytes 772
Sparse Core Ops, SparseCore 0:
  8.9 20.8 all-gather.2
  38.0 54.7 all-gather.4
